TPU v7x, 32 devices: a whole 2x2x4 slice. The times are simulated.
32 devices in a mesh: row: 8 (over y, x, core), col: 4 (over z).
Axes of the slice: x: 2, y: 2, z: 4, core: 2. Of those that a mesh axis runs over, the one named last changes fastest.
Arguments:
- sensitivity: bfloat16 [512, 24576], P(('row', 'col')), may hold values from -0.25 to 0.25
- sensor_of_row: int32 [512], P(('row', 'col')), may hold values from 0 to 127
- row_class: int32 [512], P(('row', 'col')), may hold values from 0 to 3
- sensor_precision: float32 [128], replicated, may hold values from 0.25 to 4
- class_weight: float32 [4], replicated, may hold values from 0.25 to 2.5
Outputs:
- hessian: float32 [4, 24576, 6144], P('col', 'row')
All inputs are finite; a program needn't handle non-finite values.
Results may differ from a plain program's by a relative error of at most 0.004.
Values may be sent and summed in bfloat16 or wider, within the bound.
A program may use at most 192 MiB of HBM per device.

v0:
```python
import jax
import jax.numpy as jnp
from jax import lax
from jax.sharding import PartitionSpec as P


def contract(left, right):
    return lax.dot_general(
        left, right, (((0,), (0,)), ((), ())), preferred_element_type=jnp.float32
    )


def shards(sensitivity, sensor_of_row, row_class, sensor_precision, class_weight):
    row_count = lax.axis_size("row")
    col_count = lax.axis_size("col")
    width = sensitivity.shape[1]
    tile_width = width // row_count
    piece_width = tile_width // col_count
    col_index = lax.axis_index("col")
    sensor_match = (
        sensor_of_row[:, None] == jnp.arange(sensor_precision.shape[0], dtype=jnp.int32)[None, :]
    )
    class_match = row_class[:, None] == jnp.arange(class_weight.shape[0], dtype=jnp.int32)[None, :]
    precision = jnp.sum(jnp.where(sensor_match, sensor_precision[None, :], 0.0), axis=1)
    quality = jnp.sum(jnp.where(class_match, class_weight[None, :], 0.0), axis=1)
    scaled = (jnp.sqrt(precision * quality)[:, None] * sensitivity.astype(jnp.float32)).astype(
        jnp.bfloat16
    )
    pieces = lax.all_to_all(scaled, ("row", "col"), split_axis=1, concat_axis=0, tiled=True)
    own_tile = lax.all_gather(pieces, "col", axis=1, tiled=True)
    my_piece = lax.dynamic_slice_in_dim(own_tile, col_index * piece_width, piece_width, 1)
    block = contract(own_tile, lax.all_gather(my_piece, "row", axis=1, tiled=True))
    return block[None]


def solution(mesh):
    return jax.shard_map(
        shards,
        mesh=mesh,
        in_specs=(P(("row", "col"), None), P(("row", "col")), P(("row", "col")), P(), P()),
        out_specs=P("col", "row", None),
        check_vma=False,
    )
```

profile of v0, /device:TPU:0, one launch (start us, length us, event | category | flops | bytes accessed | tf_op | source)
XLA Modules:
  0.0 187.6 jit_solution(11318577829438510996)
XLA Ops:
  6.5 0.0 all-gather.3.cloned.1.call-start
  6.5 0.9 select_reduce_fusion
  7.4 0.8 select_reduce_fusion.1
  8.2 1.3 multiply_convert_fusion
  9.5 0.1 copy.11
  9.6 26.8 %all_to_all.19 = bf16[16,32,768]{2,0,1:T(8,128)(2,1)} all-to-all(bf16[16,32,768]{2,0,1:T(8,128)(2,1)S(1)} %bitcast.13), channel_id=1, replica_groups=mesh['row'=8,'col'=4] {'row','col'}, dimensions={1} | all-to-all | bytes 1572864 | tf_op jit(solution)/shard_map/all_to_all | solution.py:29
  36.4 0.0 all-gather.3.cloned.1.call-update
  36.4 0.0 all-gather.5.cloned.1.call-start
  36.5 63.3 %all-gather.3.cloned.1.call-done = bf16[512,3072]{1,0:T(8,128)(2,1)} async-done(((bf16[512,768]{1,0:T(8,128)(2,1)}), bf16[512,3072]{1,0:T(8,128)(2,1)}) %all-gather.3.cloned.1.call-update) | async-done | bytes 3145744 | tf_op jit(solution)/shard_map/all_gather | solution.py:30
  99.8 2.1 %constant_dynamic-slice_fusion = bf16[512,768]{1,0:T(8,128)(2,1)} fusion(bf16[512,3072]{1,0:T(8,128)(2,1)} %all-gather.3.cloned.1.call-done, s32[]{:T(128)S(6)} %select_n.13), kind=kLoop, calls=%fused_computation.8 | loop fusion | bytes 1572868 | tf_op jit(solution)/shard_map/dynamic_slice | solution.py:31
  101.9 0.0 all-gather.5.cloned.1.call-update
  101.9 44.2 %all-gather.5.cloned.1.call-done = bf16[512,6144]{1,0:T(8,128)(2,1)} async-done(((bf16[512,768]{1,0:T(8,128)(2,1)}), bf16[512,6144]{1,0:T(8,128)(2,1)}) %all-gather.5.cloned.1.call-update) | async-done | bytes 6291472 | tf_op jit(solution)/shard_map/all_gather | solution.py:32
  146.1 34.6 %convolution_bitcast_fusion = f32[1,3072,6144]{2,1,0:T(8,128)} fusion(bf16[512,3072]{1,0:T(8,128)(2,1)} %all-gather.3.cloned.1.call-done, bf16[512,6144]{1,0:T(8,128)(2,1)} %all-gather.5.cloned.1.call-done), kind=kOutput, calls=%fused_computation | convolution fusion | flops 19327352832 | bytes 84934656 | tf_op jit(solution)/shard_map/dot_general | solution.py:8
  (1 shorter events, 0.0 us)
Async XLA Ops:
  6.5 93.3 %all-gather.3.cloned.1.call-start = ((), (), s32[]{:S(2)}) async-start(), calls=%async_computation.1 | async-start | bytes 3932160 | tf_op jit(solution)/shard_map/all_gather | solution.py:30
  36.4 109.7 %all-gather.5.cloned.1.call-start = ((), (), s32[]{:S(2)}) async-start(), calls=%async_computation.2 | async-start | bytes 7077888 | tf_op jit(solution)/shard_map/all_gather | solution.py:32
Sparse Core Ops, SparseCore 0:
  36.5 63.2 all-gather.2
  102.0 44.0 all-gather.4
where the time goes:
time: 188 us
  waiting for transfers between devices  108 us (57%)
  matrix products  34.6 us (18%)
  blocking collectives  26.8 us (14%)
  between operations  13.4 us (7%)
  other arithmetic  2.95 us (2%)
  local copies, waits for them, and re-layouts  2.11 us (1%)
    all_gather x1, waiting for transfers between devices, shards(): own_tile = lax.all_gather(pieces, 'col', axis=1, tiled=True)  63.3 us
    all_gather x1, waiting for transfers between devices, shards(): lax.all_gather(my_piece, 'row', axis=1, tiled=True)  44.2 us
    dot_general x1, matrix products, contract(): lax.dot_general(left, right, (((0,), (0,)), ((), ())), preferred_element_...  34.6 us
    all_to_all x1, blocking collectives, shards(): lax.all_to_all(scaled, ('row', 'col'), split_axis=1, concat_axis=0, tiled...  26.8 us
  transfers between devices with their start and end apart: 2, of which 2 were waited for; matrix products, arithmetic and copies ran while one was open for 0% of the time, Pallas kernels for 0%

commit v1 on v0

v1 whole, which is shorter than its diff:
```python
import functools

import jax
import jax.numpy as jnp
from jax import lax
from jax.experimental import pallas as pl
from jax.experimental.pallas import tpu as pltpu
from jax.sharding import PartitionSpec as P

MESH = pl.DeviceIdType.MESH


def contract(left, right):
    return lax.dot_general(
        left, right, (((0,), (0,)), ((), ())), preferred_element_type=jnp.float32
    )


def scale_rows(sensitivity, sensor_of_row, row_class, sensor_precision, class_weight):
    sensor_match = (
        sensor_of_row[:, None] == jnp.arange(sensor_precision.shape[0], dtype=jnp.int32)[None, :]
    )
    class_match = row_class[:, None] == jnp.arange(class_weight.shape[0], dtype=jnp.int32)[None, :]
    precision = jnp.sum(jnp.where(sensor_match, sensor_precision[None, :], 0.0), axis=1)
    quality = jnp.sum(jnp.where(class_match, class_weight[None, :], 0.0), axis=1)
    return (jnp.sqrt(precision * quality)[:, None] * sensitivity.astype(jnp.float32)).astype(
        jnp.bfloat16
    )


def general(row_count, col_count, scaled):
    piece_width = scaled.shape[1] // (row_count * col_count)
    pieces = lax.all_to_all(scaled, ("row", "col"), split_axis=1, concat_axis=0, tiled=True)
    own_tile = lax.all_gather(pieces, "col", axis=1, tiled=True)
    col_index = lax.axis_index("col")
    my_piece = lax.dynamic_slice_in_dim(own_tile, col_index * piece_width, piece_width, 1)
    return contract(own_tile, lax.all_gather(my_piece, "row", axis=1, tiled=True))


def gather_kernel(
    rows, cols, x_ref, tile_ref, panel_ref,
    own_sem, a_send, a_recv, up_send, down_send, z_recv, keep_sem, p_send, pair_send, p_recv,
):
    r = lax.axis_index("row")
    c = lax.axis_index("col")
    pair = r + 1 - 2 * (r % 2)
    depth = x_ref.shape[0]
    width = x_ref.shape[1] // (rows * cols)
    tile_width = width * cols
    share = depth * rows

    def peer(k):
        return (r + k) % rows

    def other(k):
        return (r + 2 * k) % rows

    barrier = pltpu.get_barrier_semaphore()
    for k in range(1, rows):
        pl.semaphore_signal(barrier, inc=1, device_id=(peer(k), c), device_id_type=MESH)

    @pl.when(c > 0)
    def _():
        pl.semaphore_signal(barrier, inc=1, device_id=(r, c - 1), device_id_type=MESH)

    @pl.when(c < cols - 1)
    def _():
        pl.semaphore_signal(barrier, inc=1, device_id=(r, c + 1), device_id_type=MESH)

    neighbours = (c + cols - 1) // cols + (2 * cols - 2 - c) // cols
    pl.semaphore_wait(barrier, rows - 1 + neighbours)

    def piece_at(q):
        return (q + cols - 1) % cols

    def columns(p):
        return pl.ds(pl.multiple_of(p * width, width), width)

    def deal(k, p):
        to = peer(k)
        return pltpu.make_async_remote_copy(
            src_ref=x_ref.at[:, pl.ds(pl.multiple_of(to * tile_width + p * width, width), width)],
            dst_ref=tile_ref.at[c, pl.ds(pl.multiple_of(r * depth, depth), depth), columns(p)],
            send_sem=a_send.at[k, p],
            recv_sem=a_recv.at[k, p],
            device_id=(to, c),
            device_id_type=MESH,
        )

    def dealt(k, p):
        source = (r + rows - k) % rows
        return pltpu.make_async_remote_copy(
            src_ref=x_ref.at[:, columns(p)],
            dst_ref=tile_ref.at[c, pl.ds(pl.multiple_of(source * depth, depth), depth), columns(p)],
            send_sem=a_send.at[k, p],
            recv_sem=a_recv.at[k, p],
            device_id=(source, c),
            device_id_type=MESH,
        )

    def own_copy():
        return pltpu.make_async_copy(
            x_ref.at[:, pl.ds(pl.multiple_of(r * tile_width, tile_width), tile_width)],
            tile_ref.at[c, pl.ds(pl.multiple_of(r * depth, depth), depth), :],
            own_sem,
        )

    def along(z, p, sem, to):
        block = tile_ref.at[z, :, columns(p)]
        return pltpu.make_async_remote_copy(
            src_ref=block,
            dst_ref=block,
            send_sem=sem.at[z, p],
            recv_sem=z_recv.at[z, p],
            device_id=(r, to),
            device_id_type=MESH,
        )

    def slot(source, z):
        return panel_ref.at[source, pl.ds(pl.multiple_of(z * share, share), share), :]

    def keep(z):
        return pltpu.make_async_copy(tile_ref.at[z, :, columns(c)], slot(r, z), keep_sem.at[z])

    def spread(k, z):
        return pltpu.make_async_remote_copy(
            src_ref=tile_ref.at[z, :, columns(c)],
            dst_ref=slot(r, z),
            send_sem=p_send.at[k, z],
            recv_sem=p_recv.at[r, z],
            device_id=(other(k), c),
            device_id_type=MESH,
        )

    def share_own(z):
        return pltpu.make_async_remote_copy(
            src_ref=tile_ref.at[z, :, columns(c)],
            dst_ref=slot(r, z),
            send_sem=pair_send.at[0, z],
            recv_sem=p_recv.at[r, z],
            device_id=(pair, c),
            device_id_type=MESH,
        )

    def pass_on(k, z):
        source = other(k)
        return pltpu.make_async_remote_copy(
            src_ref=slot(source, z),
            dst_ref=slot(source, z),
            send_sem=pair_send.at[k, z],
            recv_sem=p_recv.at[source, z],
            device_id=(pair, c),
            device_id_type=MESH,
        )

    def start_spread(z):
        for k in range(1, rows // 2):
            spread(k, z).start()
        share_own(z).start()
        keep(z).start()

    def hand_to_pair(z):
        for k in range(1, rows // 2):
            copy = pass_on(k, z)
            copy.wait_recv()
            copy.start()

    own_copy().start()

    def start_deal(q, carry):
        p = piece_at(q)
        for k in range(1, rows):
            deal(k, p).start()
        return carry

    lax.fori_loop(0, cols, start_deal, 0)
    own_copy().wait()

    def first(q, carry):
        p = piece_at(q)
        for k in range(1, rows):
            dealt(k, p).wait_recv()

        @pl.when(c < cols - 1)
        def _():
            along(c, p, up_send, c + 1).start()

        @pl.when(c > 0)
        def _():
            along(c, p, down_send, c - 1).start()

        @pl.when(p == c)
        def _():
            start_spread(c)

        return carry

    lax.fori_loop(0, cols, first, 0)

    for distance in range(1, cols):
        below = c - distance
        above = c + distance

        def step(q, carry, below=below, above=above, distance=distance):
            p = piece_at(q)

            @pl.when(below >= 0)
            def _():
                along(below, p, up_send, c).wait_recv()

                @pl.when(c < cols - 1)
                def _():
                    along(below, p, up_send, c + 1).start()

                @pl.when(p == c)
                def _():
                    start_spread(below)

            @pl.when(above < cols)
            def _():
                along(above, p, down_send, c).wait_recv()

                @pl.when(c > 0)
                def _():
                    along(above, p, down_send, c - 1).start()

                @pl.when(p == c)
                def _():
                    start_spread(above)

            return carry

        lax.fori_loop(0, cols, step, 0)
        if distance == 1:
            hand_to_pair(c)
        else:

            @pl.when(c - distance + 1 >= 0)
            def _(distance=distance):
                hand_to_pair(c - distance + 1)

            @pl.when(c + distance - 1 < cols)
            def _(distance=distance):
                hand_to_pair(c + distance - 1)

    @pl.when(c == cols - 1)
    def _():
        hand_to_pair(0)

    @pl.when(c == 0)
    def _():
        hand_to_pair(cols - 1)

    def finish(z, carry):
        keep(z).wait()
        for k in range(rows // 2):
            source = (pair + 2 * k) % rows
            pltpu.make_async_remote_copy(
                src_ref=slot(source, z),
                dst_ref=slot(source, z),
                send_sem=pair_send.at[k, z],
                recv_sem=p_recv.at[source, z],
                device_id=(pair, c),
                device_id_type=MESH,
            ).wait_recv()
        for k in range(1, rows):
            deal(k, z).wait_send()
        for k in range(1, rows // 2):
            spread(k, z).wait_send()
            pass_on(k, z).wait_send()
        share_own(z).wait_send()

        def sent(p, carry):
            @pl.when((z <= c) & (c < cols - 1))
            def _():
                along(z, p, up_send, c + 1).wait_send()

            @pl.when((z >= c) & (c > 0))
            def _():
                along(z, p, down_send, c - 1).wait_send()

            return carry

        return lax.fori_loop(0, cols, sent, carry)

    lax.fori_loop(0, cols, finish, 0)


def gather(rows, cols, scaled):
    depth, total = scaled.shape
    width = total // (rows * cols)
    dma = pltpu.SemaphoreType.DMA
    return pl.pallas_call(
        functools.partial(gather_kernel, rows, cols),
        out_shape=(
            jax.ShapeDtypeStruct((cols, depth * rows, width * cols), jnp.bfloat16),
            jax.ShapeDtypeStruct((rows, depth * rows * cols, width), jnp.bfloat16),
        ),
        in_specs=[pl.BlockSpec(memory_space=pl.ANY)],
        out_specs=(pl.BlockSpec(memory_space=pl.ANY), pl.BlockSpec(memory_space=pl.ANY)),
        scratch_shapes=[
            dma,
            dma((rows, cols)),
            dma((rows, cols)),
            dma((cols, cols)),
            dma((cols, cols)),
            dma((cols, cols)),
            dma((cols,)),
            dma((rows // 2, cols)),
            dma((rows // 2, cols)),
            dma((rows, cols)),
        ],
        compiler_params=pltpu.CompilerParams(collective_id=0, has_side_effects=True),
    )(scaled)


def product_kernel(tile_ref, panel_ref, out_ref, flipped):
    p = pl.program_id(0)
    i = pl.program_id(1)
    shares, share, width = tile_ref.shape

    @pl.when(p == 0)
    def _():
        for s in range(shares):
            flipped[i, :, s * share : (s + 1) * share] = tile_ref[s].T

    out_ref[0] = jnp.dot(flipped[i], panel_ref[0], preferred_element_type=jnp.float32)


def product(tile, panel):
    shares, share, height = tile.shape
    count, depth, width = panel.shape
    steps = height // width
    return pl.pallas_call(
        product_kernel,
        grid=(count, steps),
        out_shape=jax.ShapeDtypeStruct((1, height, count * width), jnp.float32),
        in_specs=[
            pl.BlockSpec(
                (shares, share, width), lambda p, i: (0, 0, jnp.where(p == 0, i, steps - 1))
            ),
            pl.BlockSpec((1, depth, width), lambda p, i: (p, 0, 0)),
        ],
        out_specs=pl.BlockSpec((1, width, width), lambda p, i: (0, i, p)),
        scratch_shapes=[pltpu.VMEM((steps, width, depth), jnp.bfloat16)],
        compiler_params=pltpu.CompilerParams(vmem_limit_bytes=60 * 2**20),
        cost_estimate=pl.CostEstimate(
            flops=2 * height * count * width * depth,
            bytes_accessed=4 * height * count * width,
            transcendentals=0,
        ),
    )(tile, panel)


def shards(rows, cols, sensitivity, *parameters):
    scaled = scale_rows(sensitivity, *parameters)
    depth, total = scaled.shape
    if rows == 8 and cols == 4 and depth % 16 == 0 and total % (rows * cols * 128) == 0:
        tile, panel = gather(rows, cols, scaled)
        return product(tile, panel)
    return general(rows, cols, scaled)[None]


def solution(mesh):
    return jax.shard_map(
        functools.partial(shards, mesh.shape["row"], mesh.shape["col"]),
        mesh=mesh,
        in_specs=(P(("row", "col"), None), P(("row", "col")), P(("row", "col")), P(), P()),
        out_specs=P("col", "row", None),
        check_vma=False,
    )
```

time: 188 us -> 113 us (0.60)
  Pallas kernels: 0 us -> 109 us
  waiting for transfers between devices: 108 us -> 0 us
  matrix products: 34.6 us -> 0 us
  blocking collectives: 26.8 us -> 0 us
  between operations: 13.4 us -> 0.01 us
  local copies, waits for them, and re-layouts: 2.11 us -> 0 us
    pallas_call x0 -> x2, Pallas kernels: none -> 109 us  [the longest x1 68.5 us: gather(): pl.pallas_call(functools.partial(gather_kernel, rows, cols), out_shape=(j...]
    all_gather x2 -> x0, waiting for transfers between devices: 108 us -> none  [the longest x1 63.3 us: shards(): own_tile = lax.all_gather(pieces, 'col', axis=1, tiled=True)]
    dot_general x1 -> x0, matrix products: 34.6 us -> none  [contract(): lax.dot_general(left, right, (((0,), (0,)), ((), ())), preferred_element_...]
    all_to_all x1 -> x0, blocking collectives: 26.8 us -> none  [shards(): lax.all_to_all(scaled, ('row', 'col'), split_axis=1, concat_axis=0, tiled...]
    dynamic_slice x1 -> x0, local copies, waits for them, and re-layouts: 2.06 us -> none  [shards(): lax.dynamic_slice_in_dim(own_tile, col_index * piece_width, piece_width, 1)]
  transfers between devices with their start and end apart: 2 -> 0, of which waited for: 2 -> 0; matrix products, arithmetic and copies ran while one was open for 0% -> 0% of each run, Pallas kernels for 0% -> 0%
where the time goes in v1:
time: 113 us
  Pallas kernels  109 us (96%)
  other arithmetic  3.83 us (3%)
    pallas_call x1, Pallas kernels, gather(): pl.pallas_call(functools.partial(gather_kernel, rows, cols), out_shape=(j...  68.5 us
    pallas_call x1, Pallas kernels, product(): pl.pallas_call(product_kernel, grid=(count, steps), out_shape=jax.ShapeDt...  40.3 us

profile of v1, /device:TPU:0, one launch (start us, length us, event | category | flops | bytes accessed | tf_op | source)
XLA Modules:
  0.0 112.7 jit_solution(5801176324794264391)
XLA Ops:
  0.0 0.9 select_reduce_fusion
  0.9 0.8 select_reduce_fusion.1
  1.6 2.2 %multiply_convert_fusion.x_ref = bf16[16,24576]{1,0:T(8,128)(2,1)} fusion(bf16[16,24576]{1,0:T(8,128)(2,1)} %param.5, f32[16]{0:T(128)S(1)} %multiply_sqrt_fusion), kind=kLoop, calls=%fused_computation | loop fusion | flops 1179648 | bytes 1572928 | tf_op jit(solution)/shard_map/convert_element_type | solution.py:26
  3.8 68.5 %shard_map.55 = (bf16[4,128,3072]{2,1,0:T(8,128)(2,1)}, bf16[8,512,768]{2,1,0:T(8,128)(2,1)}) custom-call(bf16[16,24576]{1,0:T(8,128)(2,1)} %multiply_convert_fusion.x_ref), custom_call_target="tpu_custom_call" | custom-call | tf_op jit(solution)/shard_map/pallas_call | solution.py:293
  72.3 40.3 %shard_map.56 = f32[1,3072,6144]{2,1,0:T(8,128)} custom-call(bf16[4,128,3072]{2,1,0:T(8,128)(2,1)} %get-tuple-element.7.tile_ref, bf16[8,512,768]{2,1,0:T(8,128)(2,1)} %get-tuple-element.8.panel_ref), custom_call_target="tpu_custom_call" | custom-call | flops 19327352832 | bytes 75497472 | tf_op jit(solution)/shard_map/pallas_call | solution.py:334
  (1 shorter events, 0.0 us)

commit v2 on v1

--- a/solution.py
+++ b/solution.py
@@ -316,33 +316,29 @@
 
 def product_kernel(tile_ref, panel_ref, out_ref, flipped):
     p = pl.program_id(0)
-    i = pl.program_id(1)
-    shares, share, width = tile_ref.shape
+    shares, share, height = tile_ref.shape
 
     @pl.when(p == 0)
     def _():
         for s in range(shares):
-            flipped[i, :, s * share : (s + 1) * share] = tile_ref[s].T
-
-    out_ref[0] = jnp.dot(flipped[i], panel_ref[0], preferred_element_type=jnp.float32)
+            flipped[:, s * share : (s + 1) * share] = tile_ref[s].T
+
+    out_ref[0] = jnp.dot(flipped[...], panel_ref[0], preferred_element_type=jnp.float32)
 
 
 def product(tile, panel):
     shares, share, height = tile.shape
     count, depth, width = panel.shape
-    steps = height // width
     return pl.pallas_call(
         product_kernel,
-        grid=(count, steps),
+        grid=(count,),
         out_shape=jax.ShapeDtypeStruct((1, height, count * width), jnp.float32),
         in_specs=[
-            pl.BlockSpec(
-                (shares, share, width), lambda p, i: (0, 0, jnp.where(p == 0, i, steps - 1))
-            ),
-            pl.BlockSpec((1, depth, width), lambda p, i: (p, 0, 0)),
+            pl.BlockSpec((shares, share, height), lambda p: (0, 0, 0)),
+            pl.BlockSpec((1, depth, width), lambda p: (p, 0, 0)),
         ],
-        out_specs=pl.BlockSpec((1, width, width), lambda p, i: (0, i, p)),
-        scratch_shapes=[pltpu.VMEM((steps, width, depth), jnp.bfloat16)],
+        out_specs=pl.BlockSpec((1, height, width), lambda p: (0, 0, p)),
+        scratch_shapes=[pltpu.VMEM((height, depth), jnp.bfloat16)],
         compiler_params=pltpu.CompilerParams(vmem_limit_bytes=60 * 2**20),
         cost_estimate=pl.CostEstimate(
             flops=2 * height * count * width * depth,

time: 113 us -> 104 us (0.920)
  Pallas kernels: 109 us -> 100 us
    pallas_call x1, Pallas kernels: 40.3 us -> 31.6 us  [product(): pl.pallas_call(product_kernel, grid=(count,), out_shape=jax.ShapeDtypeStr...]
where the time goes in v2:
time: 104 us
  Pallas kernels  100 us (96%)
  other arithmetic  3.83 us (4%)
    pallas_call x1, Pallas kernels, gather(): pl.pallas_call(functools.partial(gather_kernel, rows, cols), out_shape=(j...  68.5 us
    pallas_call x1, Pallas kernels, product(): pl.pallas_call(product_kernel, grid=(count,), out_shape=jax.ShapeDtypeStr...  31.6 us
    convert_element_type x1, other arithmetic, scale_rows(): (jnp.sqrt(precision * quality)[:, None] * sensitivity.astype(jnp.float32)...  2.21 us

profile of v2, /device:TPU:0, one launch (start us, length us, event | category | flops | bytes accessed | tf_op | source)
XLA Modules:
  0.0 103.9 jit_solution(7526114467907637081)
XLA Ops:
  0.0 0.9 select_reduce_fusion
  0.9 0.8 select_reduce_fusion.1
  1.6 2.2 %multiply_convert_fusion.x_ref = bf16[16,24576]{1,0:T(8,128)(2,1)} fusion(bf16[16,24576]{1,0:T(8,128)(2,1)} %param.5, f32[16]{0:T(128)S(1)} %multiply_sqrt_fusion), kind=kLoop, calls=%fused_computation | loop fusion | flops 1179648 | bytes 1572928 | tf_op jit(solution)/shard_map/convert_element_type | solution.py:26
  3.8 68.5 %shard_map.55 = (bf16[4,128,3072]{2,1,0:T(8,128)(2,1)}, bf16[8,512,768]{2,1,0:T(8,128)(2,1)}) custom-call(bf16[16,24576]{1,0:T(8,128)(2,1)} %multiply_convert_fusion.x_ref), custom_call_target="tpu_custom_call" | custom-call | tf_op jit(solution)/shard_map/pallas_call | solution.py:293
  72.3 31.6 %shard_map.56 = f32[1,3072,6144]{2,1,0:T(8,128)} custom-call(bf16[4,128,3072]{2,1,0:T(8,128)(2,1)} %get-tuple-element.7.tile_ref, bf16[8,512,768]{2,1,0:T(8,128)(2,1)} %get-tuple-element.8.panel_ref), custom_call_target="tpu_custom_call" | custom-call | flops 19327352832 | bytes 75497472 | tf_op jit(solution)/shard_map/pallas_call | solution.py:332
  (1 shorter events, 0.0 us)

commit v3 on v2

--- a/solution.py
+++ b/solution.py
@@ -38,8 +38,8 @@
 
 
 def gather_kernel(
-    rows, cols, x_ref, tile_ref, panel_ref,
-    own_sem, a_send, a_recv, up_send, down_send, z_recv, keep_sem, p_send, pair_send, p_recv,
+    rows, cols, raw_ref, sensor_ref, class_ref, precision_ref, quality_ref, tile_ref, panel_ref,
+    x_ref, own_sem, a_send, a_recv, up_send, down_send, z_recv, keep_sem, p_send, pair_send, p_recv,
 ):
     r = lax.axis_index("row")
     c = lax.axis_index("col")
@@ -66,6 +66,21 @@
     @pl.when(c < cols - 1)
     def _():
         pl.semaphore_signal(barrier, inc=1, device_id=(r, c + 1), device_id_type=MESH)
+
+    def pick(index_ref, table_ref):
+        spots = lax.broadcasted_iota(jnp.int32, (depth, table_ref.shape[1]), 1)
+        return jnp.sum(
+            jnp.where(index_ref[...] == spots, table_ref[...], 0.0), axis=1, keepdims=True
+        )
+
+    root = jnp.sqrt(pick(sensor_ref, precision_ref) * pick(class_ref, quality_ref))
+
+    def scale(i, carry):
+        part = pl.ds(pl.multiple_of(i * width, width), width)
+        x_ref[:, part] = (root * raw_ref[:, part].astype(jnp.float32)).astype(jnp.bfloat16)
+        return carry
+
+    lax.fori_loop(0, rows * cols, scale, 0)
 
     neighbours = (c + cols - 1) // cols + (2 * cols - 2 - c) // cols
     pl.semaphore_wait(barrier, rows - 1 + neighbours)
@@ -286,8 +301,8 @@
     lax.fori_loop(0, cols, finish, 0)
 
 
-def gather(rows, cols, scaled):
-    depth, total = scaled.shape
+def gather(rows, cols, sensitivity, sensor_of_row, row_class, sensor_precision, class_weight):
+    depth, total = sensitivity.shape
     width = total // (rows * cols)
     dma = pltpu.SemaphoreType.DMA
     return pl.pallas_call(
@@ -296,9 +311,10 @@
             jax.ShapeDtypeStruct((cols, depth * rows, width * cols), jnp.bfloat16),
             jax.ShapeDtypeStruct((rows, depth * rows * cols, width), jnp.bfloat16),
         ),
-        in_specs=[pl.BlockSpec(memory_space=pl.ANY)],
+        in_specs=[pl.BlockSpec(memory_space=pltpu.VMEM)] * 5,
         out_specs=(pl.BlockSpec(memory_space=pl.ANY), pl.BlockSpec(memory_space=pl.ANY)),
         scratch_shapes=[
+            pltpu.VMEM((depth, total), jnp.bfloat16),
             dma,
             dma((rows, cols)),
             dma((rows, cols)),
@@ -310,8 +326,16 @@
             dma((rows // 2, cols)),
             dma((rows, cols)),
         ],
-        compiler_params=pltpu.CompilerParams(collective_id=0, has_side_effects=True),
-    )(scaled)
+        compiler_params=pltpu.CompilerParams(
+            collective_id=0, has_side_effects=True, vmem_limit_bytes=58 * 2**20
+        ),
+    )(
+        sensitivity,
+        sensor_of_row[:, None],
+        row_class[:, None],
+        sensor_precision[None, :],
+        class_weight[None, :],
+    )
 
 
 def product_kernel(tile_ref, panel_ref, out_ref, flipped):
@@ -349,12 +373,11 @@
 
 
 def shards(rows, cols, sensitivity, *parameters):
-    scaled = scale_rows(sensitivity, *parameters)
-    depth, total = scaled.shape
+    depth, total = sensitivity.shape
     if rows == 8 and cols == 4 and depth % 16 == 0 and total % (rows * cols * 128) == 0:
-        tile, panel = gather(rows, cols, scaled)
+        tile, panel = gather(rows, cols, sensitivity, *parameters)
         return product(tile, panel)
-    return general(rows, cols, scaled)[None]
+    return general(rows, cols, scale_rows(sensitivity, *parameters))[None]
 
 
 def solution(mesh):

time: 104 us -> 104 us (level)
  other arithmetic: 3.83 us -> 0 us
  local copies, waits for them, and re-layouts: 0 us -> 2.65 us
    broadcast_in_dim x0 -> x2, local copies, waits for them, and re-layouts: none -> 2.65 us  [the longest x1 1.33 us: gather(): sensor_of_row[:, None]]
    convert_element_type x1 -> x0, other arithmetic: 2.21 us -> none  [scale_rows(): (jnp.sqrt(precision * quality)[:, None] * sensitivity.astype(jnp.float32)...]
    reduce_sum x2 -> x0, other arithmetic: 1.61 us -> none  [the longest x1 0.85 us: scale_rows(): jnp.sum(jnp.where(sensor_match, sensor_precision[None, :], 0.0), axis=1)]
where the time goes in v3:
time: 104 us
  Pallas kernels  101 us (97%)
  local copies, waits for them, and re-layouts  2.65 us (3%)
    pallas_call x1, Pallas kernels, gather(): pl.pallas_call(functools.partial(gather_kernel, rows, cols), out_shape=(j...  69.5 us
    pallas_call x1, Pallas kernels, product(): pl.pallas_call(product_kernel, grid=(count,), out_shape=jax.ShapeDtypeStr...  31.6 us

profile of v3, /device:TPU:0, one launch (start us, length us, event | category | flops | bytes accessed | tf_op | source)
XLA Modules:
  0.0 103.7 jit_solution(15528886200353792275)
XLA Ops:
  0.0 1.3 %copy.6.sensor_ref = s32[16,1]{1,0:T(8,128)} copy(s32[16,1]{0,1:T(1,128)} %bitcast.6) | data formatting | bytes 128 | tf_op jit(solution)/shard_map/broadcast_in_dim | solution.py:334
  1.3 1.3 %copy.7.class_ref = s32[16,1]{1,0:T(8,128)} copy(s32[16,1]{0,1:T(1,128)} %bitcast.7) | data formatting | bytes 128 | tf_op jit(solution)/shard_map/broadcast_in_dim | solution.py:335
  2.6 69.5 %shard_map.55 = (bf16[4,128,3072]{2,1,0:T(8,128)(2,1)}, bf16[8,512,768]{2,1,0:T(8,128)(2,1)}) custom-call(bf16[16,24576]{1,0:T(8,128)(2,1)} %raw_ref.1, s32[16,1]{1,0:T(8,128)} %copy.6.sensor_ref, s32[16,1]{1,0:T(8,128)} %copy.7.class_ref, f32[1,128]{1,0:T(1,128)} %bitcast.4, f32[1,4]{1,0:T(1,128)} %bitcast.5), custom_call_target="tpu_custom_call" | custom-call | tf_op jit(solution)/shard_map/pallas_call | solution.py:308
  72.1 31.6 %shard_map.56 = f32[1,3072,6144]{2,1,0:T(8,128)} custom-call(bf16[4,128,3072]{2,1,0:T(8,128)(2,1)} %get-tuple-element.7.tile_ref, bf16[8,512,768]{2,1,0:T(8,128)(2,1)} %get-tuple-element.8.panel_ref), custom_call_target="tpu_custom_call" | custom-call | flops 19327352832 | bytes 75497472 | tf_op jit(solution)/shard_map/pallas_call | solution.py:356
